TPU v7x, 32 devices: a whole 2x2x4 slice. The times are simulated.
32 devices in a mesh: var: 8 (over y, x, core), smp: 4 (over z).
Axes of the slice: x: 2, y: 2, z: 4, core: 2. Of those that a mesh axis runs over, the one named last changes fastest.
Arguments:
- dosages: bfloat16 [8192, 16384], P('var', 'smp'), may hold values from 0 to 2
- window_end: int32 [8192], P('var'), may hold values from 1 to 8192, as said below
Outputs:
- ld_band: float32 [8192, 512], P('var', 'smp')
Inputs may be any that keep to these rules, and one draw needn't show every extreme that they name: Nondecreasing along the variants; window_end[i] > i and window_end[i] - i - 1 <= 512, with equality for some variants of every draw; never past 8192.
All inputs are finite; a program needn't handle non-finite values.
Results may differ from a plain program's by a relative error of at most 0.0003.
Values may be sent and summed in bfloat16 or wider, within the bound.
A program may use at most 128 MiB of HBM per device.

v0:
```python
import jax
import jax.numpy as jnp
from jax import lax
from jax.sharding import PartitionSpec as P

WIN = 512


def from_behind(value, axis, by):
    devices = lax.axis_size(axis)
    pairs = [(i, i + by) for i in range(devices) if 0 <= i + by < devices]
    return lax.ppermute(value, axis, pairs)


def local(dosages, window_end):
    row_count, samples_dev = dosages.shape
    width = WIN
    smp_count = lax.axis_size("smp")
    samples = samples_dev * smp_count
    widened = dosages.astype(jnp.float32)
    moment_sums = lax.psum((jnp.sum(widened, axis=1), jnp.sum(widened * widened, axis=1)), "smp")
    average = moment_sums[0] / samples
    spread = moment_sums[1] / samples - average * average
    scaled = ((widened - average[:, None]) * lax.rsqrt(spread + 1e-06)[:, None]).astype(
        jnp.bfloat16
    )
    block_count = row_count // width
    blocks = scaled.reshape(block_count, width, samples_dev)
    diagonal = jnp.einsum("brs,bcs->brc", blocks, blocks, preferred_element_type=jnp.float32)
    adjacent = jnp.einsum(
        "brs,bcs->brc", blocks[:-1], blocks[1:], preferred_element_type=jnp.float32
    )
    first_row = lax.axis_index("var") * row_count
    leading = from_behind(blocks[0], "var", -1)
    boundary = jnp.einsum("rs,cs->rc", blocks[-1], leading, preferred_element_type=jnp.float32)
    off_diagonal = jnp.concatenate([adjacent, boundary[None]], axis=0)
    joined = jnp.concatenate([diagonal, off_diagonal], axis=2)
    flattened = jnp.pad(joined.reshape(block_count, 2 * width * width), ((0, 0), (0, width + 1)))
    banded = flattened[:, 1 : 1 + width * (2 * width + 1)].reshape(
        block_count, width, 2 * width + 1
    )[:, :, :width]
    banded = banded.reshape(row_count, width)
    summed = lax.psum(banded, "smp")
    share = width // smp_count
    summed = lax.dynamic_slice_in_dim(summed, lax.axis_index("smp") * share, share, 1)
    col_count = summed.shape[1]
    column = lax.axis_index("smp") * col_count + jnp.arange(col_count, dtype=jnp.int32)
    row_index = first_row + jnp.arange(row_count, dtype=jnp.int32)
    retain = column[None, :] < (window_end - row_index - 1)[:, None]
    return jnp.where(retain, summed / samples, jnp.float32(0.0))


def solution(mesh):
    return jax.shard_map(
        local,
        mesh=mesh,
        in_specs=(P("var", "smp"), P("var")),
        out_specs=P("var", "smp"),
        check_vma=False,
    )
```

profile of v0, /device:TPU:5, one launch (start us, length us, event | category | flops | bytes accessed | tf_op | source)
XLA Modules:
  0.0 219.3 jit_solution(17365062585655025775)
XLA Ops:
  6.5 0.0 all-reduce.4.cloned.1.call-start
  6.5 5.9 %convert_reduce_fusion = (f32[1024]{0:T(1024)S(1)}, f32[1024]{0:T(1024)S(1)}) fusion(bf16[1024,4096]{1,0:T(8,128)(2,1)} %param.2), kind=kLoop, calls=%fused_computation.2 | loop fusion | flops 16775168 | bytes 8396800 | tf_op jit(solution)/shard_map/reduce_sum | solution.py:21
  12.5 10.1 %all-reduce.1 = (f32[1024]{0:T(1024)S(1)}, f32[1024]{0:T(1024)S(1)}) all-reduce(f32[1024]{0:T(1024)S(1)} %get-tuple-element.6, f32[1024]{0:T(1024)S(1)} %get-tuple-element.5), channel_id=1, replica_groups=mesh['var'=8,'smp'=4] {'smp'}, use_global_device_ids=true, to_apply=%region_3.0 | all-reduce | flops 2048 | bytes 16384 | tf_op jit(solution)/shard_map/psum | solution.py:21
  22.6 11.0 %fusion.1 = bf16[1024,4096]{1,0:T(8,128)(2,1)} fusion(bf16[1024,4096]{1,0:T(8,128)(2,1)} %param.2, f32[1024]{0:T(1024)S(1)} %get-tuple-element.10, f32[1024]{0:T(1024)S(1)} %get-tuple-element.9), kind=kLoop, calls=%fused_computation.4 | loop fusion | flops 16777216 | bytes 16785408 | tf_op jit(solution)/shard_map/convert_element_type | solution.py:24
  33.6 0.0 copy-start
  33.6 2.6 %slice.20 = bf16[512,4096]{1,0:T(8,128)(2,1)S(1)} slice(bf16[1024,4096]{1,0:T(8,128)(2,1)} %fusion.1), slice={[0:512], [0:4096]} | slice | bytes 8388608 | tf_op jit(solution)/shard_map/slice | solution.py:31
  36.3 5.2 %collective-permute-start = (bf16[512,4096]{1,0:T(8,128)(2,1)S(1)}, bf16[512,4096]{1,0:T(8,128)(2,1)}, u32[]{:S(2)}, u32[]{:S(2)}) collective-permute-start(bf16[512,4096]{1,0:T(8,128)(2,1)S(1)} %slice.20), channel_id=1, source_target_pairs={{4,0},{8,4},{12,8},{16,12},{20,16},{24,20},{28,24},{5,1},{9,5},{13... | collective-permute-start | bytes 12582920 | tf_op jit(solution)/shard_map/ppermute | solution.py:12
  41.5 0.0 copy-done
  41.5 2.4 %fusion.7 = f32[1,512,512]{1,2,0:T(8,128)S(1)} fusion(bf16[1024,4096]{1,0:T(8,128)(2,1)S(1)} %copy-done), kind=kOutput, calls=%fused_computation.12 | convolution fusion | flops 2147483648 | bytes 9437184 | tf_op jit(solution)/shard_map/brs,bcs->brc/dot_general | solution.py:30
  43.8 9.5 %fusion.14 = f32[2,512,512]{1,2,0:T(8,128)S(1)} fusion(bf16[2,512,4096]{2,1,0:T(8,128)(2,1)} %bitcast.11), kind=kOutput, calls=%fused_computation.20 | convolution fusion | flops 4294967296 | bytes 10485760 | tf_op jit(solution)/shard_map/brs,bcs->brc/dot_general | solution.py:29
  53.3 35.3 %collective-permute-done = bf16[512,4096]{1,0:T(8,128)(2,1)} collective-permute-done((bf16[512,4096]{1,0:T(8,128)(2,1)S(1)}, bf16[512,4096]{1,0:T(8,128)(2,1)}, u32[]{:S(2)}, u32[]{:S(2)}) %collective-permute-start) | collective-permute-done | bytes 4194336 | tf_op jit(solution)/shard_map/ppermute | solution.py:12
  88.6 5.8 %fusion.10 = f32[1,512,512]{1,2,0:T(8,128)S(1)} fusion(bf16[512,4096]{1,0:T(8,128)(2,1)} %collective-permute-done, bf16[1024,4096]{1,0:T(8,128)(2,1)} %fusion.1), kind=kOutput, calls=%fused_computation.13 | convolution fusion | flops 2147483648 | bytes 9437184 | tf_op jit(solution)/shard_map/rs,cs->rc/dot_general | solution.py:35
  94.5 2.4 %maximum_maximum_fusion = f32[2,512,1024]{1,2,0:T(8,128)} fusion(f32[1,512,512]{1,2,0:T(8,128)S(1)} %fusion.10, f32[1,512,512]{1,2,0:T(8,128)S(1)} %fusion.7, f32[2,512,512]{1,2,0:T(8,128)S(1)} %fusion.14), kind=kLoop, calls=%fused_computation.7 | loop fusion | flops 2097152 | bytes 8388608 | tf_op jit(solution)/shard_map/concatenate | solution.py:37
  96.9 5.4 %copy.3 = f32[2,512,1024]{2,1,0:T(8,128)} copy(f32[2,512,1024]{1,2,0:T(8,128)} %maximum_maximum_fusion) | data formatting | bytes 8388608 | tf_op jit(solution)/shard_map/concatenate | solution.py:37
  102.3 5.4 %copy.4 = f32[1,2,512,1024]{3,1,2,0:T(2,128)S(1)} copy(f32[1,2,512,1024]{3,2,1,0:T(8,128)} %bitcast.12) | data formatting | bytes 8388608
  107.7 5.7 %pad_slice_fusion = f32[2,524800]{1,0:T(2,128)} fusion(f32[2,524288]{1,0:T(2,128)S(1)} %bitcast.13), kind=kLoop, calls=%fused_computation.6 | loop fusion | bytes 8392704 | tf_op jit(solution)/shard_map/slice | solution.py:39
  113.4 10.4 %reshape.30 = f32[2,512,1025]{2,1,0:T(8,128)} reshape(f32[2,524800]{1,0:T(2,128)} %pad_slice_fusion) | data formatting | bytes 8396800 | tf_op jit(solution)/shard_map/reshape | solution.py:39
  123.9 0.0 copy-start.1
  123.9 3.1 %slice.22 = f32[2,512,512]{2,1,0:T(8,128)} slice(f32[2,512,1025]{2,1,0:T(8,128)} %reshape.30), slice={[0:2], [0:512], [0:512]} | slice | bytes 4194304 | tf_op jit(solution)/shard_map/slice | solution.py:39
  127.0 0.0 all-reduce.4.cloned.1.call-update
  127.1 0.0 copy-done.1
  127.1 83.4 %all-reduce.4.cloned.1.call-done = f32[1024,512]{1,0:T(8,128)} async-done(((f32[1024,512]{1,0:T(8,128)}), f32[1024,512]{1,0:T(8,128)}) %all-reduce.4.cloned.1.call-update) | async-done | bytes 2097168 | tf_op jit(solution)/shard_map/psum | solution.py:43
  210.4 2.0 multiply_select_fusion
  (3 shorter events, 0.0 us)
Async XLA Ops:
  6.5 203.9 %all-reduce.4.cloned.1.call-start = ((), (), s32[]{:S(2)}) async-start(), calls=%async_computation | async-start | bytes 4194304 | tf_op jit(solution)/shard_map/psum | solution.py:43
  33.6 7.8 %copy-start = (bf16[1024,4096]{1,0:T(8,128)(2,1)S(1)}, bf16[1024,4096]{1,0:T(8,128)(2,1)}, u32[]{:S(2)}) copy-start(bf16[1024,4096]{1,0:T(8,128)(2,1)} %fusion.1) | copy-start | bytes 25165828
  36.3 52.4 %collective-permute-start = (bf16[512,4096]{1,0:T(8,128)(2,1)S(1)}, bf16[512,4096]{1,0:T(8,128)(2,1)}, u32[]{:S(2)}, u32[]{:S(2)}) collective-permute-start(bf16[512,4096]{1,0:T(8,128)(2,1)S(1)} %slice.20), channel_id=1, source_target_pairs={{4,0},{8,4},{12,8},{16,12},{20,16},{24,20},{28,24},{5,1},{9,5},{13... | collective-permute-start | bytes 12582920 | tf_op jit(solution)/shard_map/ppermute | solution.py:12
  123.9 3.2 %copy-start.1 = (s32[1024]{0:T(1024)S(1)}, s32[1024]{0:T(1024)}, u32[]{:S(2)}) copy-start(s32[1024]{0:T(1024)} %param.3) | copy-start | bytes 12292
Sparse Core Ops, SparseCore 0:
  127.2 83.2 all-reduce.3
where the time goes:
time: 221 us; the launch traced here: 219 us
  waiting for transfers between devices  119 us (54%)
  local copies, waits for them, and re-layouts  32.7 us (15%)
  other arithmetic  21.4 us (10%)
  matrix products  17.7 us (8%)
  between operations  13.5 us (6%)
  blocking collectives  10.1 us (5%)
  starting transfers between devices  5.19 us (2%)
    psum x1, waiting for transfers between devices, local(): summed = lax.psum(banded, 'smp')  83.4 us
    ppermute x1, waiting for transfers between devices, from_behind(): return lax.ppermute(value, axis, pairs)  35.3 us
    convert_element_type x1, other arithmetic, local(): ((widened - average[:, None]) * lax.rsqrt(spread + 1e-06)[:, None]).astyp...  11 us
    reshape x1, local copies, waits for them, and re-layouts, local(): flattened[:, 1:1 + width * (2 * width + 1)]  10.4 us
    psum x1, blocking collectives, local(): lax.psum((jnp.sum(widened, axis=1), jnp.sum(widened * widened, axis=1)),...  10.1 us
    dot_general x1, matrix products, local(): jnp.einsum('brs,bcs->brc', blocks, blocks, preferred_element_type=jnp.flo...  9.49 us
    slice x2, local copies, waits for them, and re-layouts, local(): flattened[:, 1:1 + width * (2 * width + 1)]  8.85 us
    reduce_sum x1, other arithmetic, local(): jnp.sum(widened, axis=1)  5.94 us
  transfers between devices with their start and end apart: 2, of which 2 were waited for; matrix products, arithmetic and copies ran while one was open for 5% of the time, Pallas kernels for 0%

commit v1 on v0

v1 whole, which is shorter than its diff:
```python
import functools

import jax
import jax.numpy as jnp
from jax import lax
from jax.experimental import pallas as pl
from jax.experimental.pallas import tpu as pltpu
from jax.sharding import PartitionSpec as P

WIN = 512
LANE = 128
SUB = 8
SPAN = WIN // LANE
MESH = pl.DeviceIdType.MESH
NT = (((1,), (1,)), ((), ()))


def kernel(
    x_ref, end_ref, out_ref,
    own, after, product, outbox, inbox, moments, moments_in, final, final_after,
    load_sem, after_send, after_recv, moment_send, moment_recv,
    final_send, final_recv, band_send, band_recv,
):
    rows, depth = own.shape
    groups = rows // LANE
    var, smp = lax.axis_index("var"), lax.axis_index("smp")
    var_count, smp_count = lax.axis_size("var"), lax.axis_size("smp")
    samples = depth * smp_count
    has_left, has_right = var > 0, var < var_count - 1

    def peer(step):
        return lax.rem(smp + step, smp_count)

    loads = [
        pltpu.make_async_copy(
            x_ref.at[pl.ds(g * LANE, LANE)], own.at[pl.ds(g * LANE, LANE)], load_sem.at[g]
        )
        for g in range(groups)
    ]
    for load in loads:
        load.start()

    barrier = pltpu.get_barrier_semaphore()
    for step in range(1, smp_count):
        pl.semaphore_signal(barrier, 1, device_id=(var, peer(step)), device_id_type=MESH)

    @pl.when(has_left)
    def _():
        pl.semaphore_signal(barrier, 1, device_id=(var - 1, smp), device_id_type=MESH)

    @pl.when(has_right)
    def _():
        pl.semaphore_signal(barrier, 1, device_id=(var + 1, smp), device_id_type=MESH)

    pl.semaphore_wait(
        barrier, smp_count - 1 + has_left.astype(jnp.int32) + has_right.astype(jnp.int32)
    )

    def after_copy(q):
        return pltpu.make_async_remote_copy(
            src_ref=x_ref.at[pl.ds(q * LANE, LANE)],
            dst_ref=after.at[pl.ds(q * LANE, LANE)],
            send_sem=after_send.at[q],
            recv_sem=after_recv.at[q],
            device_id=(var - 1, smp),
            device_id_type=MESH,
        )

    def final_copy():
        return pltpu.make_async_remote_copy(
            src_ref=final,
            dst_ref=final_after,
            send_sem=final_send,
            recv_sem=final_recv,
            device_id=(var - 1, smp),
            device_id_type=MESH,
        )

    @pl.when(has_left)
    def _():
        for q in range(SPAN):
            after_copy(q).start()

    for g in range(groups):
        loads[g].wait()

        def add(t, sums):
            tile = own[pl.ds(g * LANE, LANE), pl.ds(pl.multiple_of(t * LANE, LANE), LANE)]
            tile = tile.astype(jnp.float32)
            return sums[0] + tile, sums[1] + tile * tile

        zero = jnp.zeros((LANE, LANE), jnp.float32)
        first, second = lax.fori_loop(0, depth // LANE, add, (zero, zero), unroll=4)
        moments[pl.ds(g, 1), :] = jnp.sum(first.T, axis=0, keepdims=True)
        moments[pl.ds(groups + g, 1), :] = jnp.sum(second.T, axis=0, keepdims=True)

    def moment_copy(step):
        return pltpu.make_async_remote_copy(
            src_ref=moments,
            dst_ref=moments_in.at[step - 1],
            send_sem=moment_send.at[step - 1],
            recv_sem=moment_recv.at[step - 1],
            device_id=(var, peer(step)),
            device_id_type=MESH,
        )

    for step in range(1, smp_count):
        moment_copy(step).start()
    for step in range(1, smp_count):
        moment_copy(step).wait()
    total = moments[...]
    for step in range(1, smp_count):
        total = total + moments_in[step - 1]
    average = total[:groups] / samples
    spread = total[groups:] / samples - average * average
    final[pl.ds(0, groups), :] = average
    final[pl.ds(groups, groups), :] = lax.rsqrt(spread + 1e-06)

    @pl.when(has_left)
    def _():
        final_copy().start()

    def column(row):
        return jnp.broadcast_to(row, (LANE, LANE)).T

    def standardize(held, g, stats):
        shift = column(stats[pl.ds(g, 1), :])
        scale = column(stats[pl.ds(groups + g, 1), :])

        @pl.loop(0, depth // LANE, unroll=4)
        def _(t):
            at = (pl.ds(g * LANE, LANE), pl.ds(pl.multiple_of(t * LANE, LANE), LANE))
            held[at] = ((held[at].astype(jnp.float32) - shift) * scale).astype(jnp.bfloat16)

    def band_copy(g, step):
        return pltpu.make_async_remote_copy(
            src_ref=outbox.at[g, peer(step)],
            dst_ref=inbox.at[g, step - 1],
            send_sem=band_send.at[g, step - 1],
            recv_sem=band_recv.at[g, step - 1],
            device_id=(var, peer(step)),
            device_id_type=MESH,
        )

    def finish_group(g):
        width, share = WIN + LANE, WIN // smp_count
        for top in range(0, LANE, SUB):
            value = pltpu.roll(product[g, pl.ds(top, SUB), :], width - 1 - top, 1)
            line = lax.broadcasted_iota(jnp.int32, (SUB, width), 0)
            for bit in range(3):
                moved = pltpu.roll(value, width - (1 << bit), 1)
                value = jnp.where((line >> bit) & 1 == 1, moved, value)
            for part in range(smp_count):
                outbox[g, part, pl.ds(top, SUB), :] = value[:, part * share : (part + 1) * share]
        for step in range(1, smp_count):
            band_copy(g, step).start()

    def place(value, row, col):
        for i in range(value.shape[0] // LANE):
            for j in range(value.shape[1] // LANE):
                g, c = row + i, col + j - row - i
                if 0 <= c <= SPAN:
                    product[g, :, pl.ds(c * LANE, LANE)] = value[
                        i * LANE : (i + 1) * LANE, j * LANE : (j + 1) * LANE
                    ]

    def dot(left, right):
        return lax.dot_general(left, right, NT, preferred_element_type=jnp.float32)

    for g in range(groups):
        standardize(own, g, final)
    for g in range(0, groups, 2):
        for c in range(g, min(g + SPAN + 2, groups), 2):
            value = dot(own[pl.ds(g * LANE, 2 * LANE), :], own[pl.ds(c * LANE, 2 * LANE), :])
            place(value, g, c)
        for done in range(g, g + 2):
            if done + SPAN < groups:
                finish_group(done)

    @pl.when(has_right)
    def _():
        final_copy().wait_recv()

    @pl.when(jnp.logical_not(has_right))
    def _():
        final_after[...] = jnp.zeros_like(final_after)
        after[...] = jnp.zeros_like(after)

    for q in range(SPAN):
        @pl.when(has_right)
        def _():
            after_copy(q).wait_recv()

        standardize(after, q, final_after)
        row = groups - SPAN + q
        value = dot(own[pl.ds(row * LANE, (SPAN - q) * LANE), :], after[pl.ds(q * LANE, LANE), :])
        place(value, row, groups + q)
        finish_group(row)

    lane = lax.broadcasted_iota(jnp.int32, (LANE, LANE), 1)
    line = lax.broadcasted_iota(jnp.int32, (LANE, LANE), 0)
    for g in range(groups):
        for step in range(1, smp_count):
            band_copy(g, step).wait()
        total = outbox[g, smp]
        for step in range(1, smp_count):
            total = total + inbox[g, step - 1]
        end = column(end_ref[pl.ds(g, 1), :].astype(jnp.float32)).astype(jnp.int32)
        index = var * rows + g * LANE + line
        retain = smp * LANE + lane < end - index - 1
        out_ref[pl.ds(g * LANE, LANE), :] = jnp.where(retain, total / samples, 0.0)

    @pl.when(has_left)
    def _():
        final_copy().wait_send()
        for q in range(SPAN):
            after_copy(q).wait_send()


def local(dosages, window_end):
    rows, depth = dosages.shape
    smp_count = lax.axis_size("smp")
    groups = rows // LANE
    share = WIN // smp_count
    dma = pltpu.SemaphoreType.DMA
    return pl.pallas_call(
        kernel,
        out_shape=jax.ShapeDtypeStruct((rows, share), jnp.float32),
        in_specs=[pl.BlockSpec(memory_space=pl.ANY), pl.BlockSpec(memory_space=pltpu.VMEM)],
        out_specs=pl.BlockSpec(memory_space=pltpu.VMEM),
        scratch_shapes=[
            pltpu.VMEM((rows, depth), jnp.bfloat16),
            pltpu.VMEM((WIN, depth), jnp.bfloat16),
            pltpu.VMEM((groups, LANE, WIN + LANE), jnp.float32),
            pltpu.VMEM((groups, smp_count, LANE, share), jnp.float32),
            pltpu.VMEM((groups, smp_count - 1, LANE, share), jnp.float32),
            pltpu.VMEM((2 * groups, LANE), jnp.float32),
            pltpu.VMEM((smp_count - 1, 2 * groups, LANE), jnp.float32),
            pltpu.VMEM((2 * groups, LANE), jnp.float32),
            pltpu.VMEM((2 * groups, LANE), jnp.float32),
            dma((groups,)),
            dma((SPAN,)),
            dma((SPAN,)),
            dma((smp_count - 1,)),
            dma((smp_count - 1,)),
            dma,
            dma,
            dma((groups, smp_count - 1)),
            dma((groups, smp_count - 1)),
        ],
        compiler_params=pltpu.CompilerParams(
            collective_id=0, has_side_effects=True, vmem_limit_bytes=48 * 1024 * 1024
        ),
    )(dosages, window_end.reshape(groups, LANE))


def solution(mesh):
    return jax.shard_map(
        local,
        mesh=mesh,
        in_specs=(P("var", "smp"), P("var")),
        out_specs=P("var", "smp"),
        check_vma=False,
    )
```

time: 221 us -> 69.9 us (0.32)
  waiting for transfers between devices: 119 us -> 0 us
  Pallas kernels: 0 us -> 67.4 us
  local copies, waits for them, and re-layouts: 32.7 us -> 1.48 us
  other arithmetic: 21.4 us -> 0 us
  matrix products: 17.7 us -> 0 us
  between operations: 13.5 us -> 0.01 us
  blocking collectives: 10.1 us -> 0 us
  starting transfers between devices: 5.19 us -> 0 us
    psum x1 -> x0, waiting for transfers between devices: 83.4 us -> none  [local(): summed = lax.psum(banded, 'smp')]
    pallas_call x0 -> x1, Pallas kernels: none -> 67.4 us  [local(): pl.pallas_call(kernel, out_shape=jax.ShapeDtypeStruct((rows, share), jnp....]
    ppermute x1 -> x0, waiting for transfers between devices: 35.3 us -> none  [from_behind(): return lax.ppermute(value, axis, pairs)]
    dot_general x3 -> x0, matrix products: 17.7 us -> none  [the longest x1 9.49 us: local(): jnp.einsum('brs,bcs->brc', blocks, blocks, preferred_element_type=jnp.flo...]
    slice x3 -> x0, local copies, waits for them, and re-layouts: 11.5 us -> none  [the longest x2 8.85 us: local(): flattened[:, 1:1 + width * (2 * width + 1)]]
    convert_element_type x1 -> x0, other arithmetic: 11 us -> none  [local(): ((widened - average[:, None]) * lax.rsqrt(spread + 1e-06)[:, None]).astyp...]
    reshape x1 -> x0, local copies, waits for them, and re-layouts: 10.4 us -> none  [local(): flattened[:, 1:1 + width * (2 * width + 1)]]
    psum x1 -> x0, blocking collectives: 10.1 us -> none  [local(): lax.psum((jnp.sum(widened, axis=1), jnp.sum(widened * widened, axis=1)),...]
  transfers between devices with their start and end apart: 2 -> 0, of which waited for: 2 -> 0; matrix products, arithmetic and copies ran while one was open for 5% -> 0% of each run, Pallas kernels for 0% -> 0%
where the time goes in v1:
time: 69.9 us; the launch traced here: 68.9 us
  Pallas kernels  67.4 us (96%)
  local copies, waits for them, and re-layouts  1.48 us (2%)
    pallas_call x1, Pallas kernels, local(): pl.pallas_call(kernel, out_shape=jax.ShapeDtypeStruct((rows, share), jnp....  67.4 us
    unnamed x3, local copies, waits for them, and re-layouts  1.48 us

profile of v1, /device:TPU:5, one launch (start us, length us, event | category | flops | bytes accessed | tf_op | source)
XLA Modules:
  0.0 68.9 jit_solution(11775135492544665529)
XLA Ops:
  0.0 0.0 copy-start
  0.0 0.7 copy-done
  0.7 67.4 %shard_map.28 = f32[1024,128]{1,0:T(8,128)S(1)} custom-call(bf16[1024,4096]{1,0:T(8,128)(2,1)} %x_ref.1, s32[8,128]{1,0:T(8,128)S(1)} %bitcast.1), custom_call_target="tpu_custom_call" | custom-call | tf_op jit(solution)/shard_map/pallas_call | solution.py:226
  68.1 0.8 %copy.4 = f32[1024,128]{1,0:T(8,128)} copy(f32[1024,128]{1,0:T(8,128)S(1)} %shard_map.28) | data formatting | bytes 1048576
Async XLA Ops:
  0.0 0.7 copy-start

commit v2 on v1

--- a/solution.py
+++ b/solution.py
@@ -17,9 +17,9 @@
 
 def kernel(
     x_ref, end_ref, out_ref,
-    own, after, product, outbox, inbox, moments, moments_in, final, final_after,
-    load_sem, after_send, after_recv, moment_send, moment_recv,
-    final_send, final_recv, band_send, band_recv,
+    own, after, before, lent, product, outbox, inbox, relayed, moments, moments_in, final, final_after, final_before,
+    load_sem, after_send, after_recv, before_send, before_recv, lent_send, lent_recv, moment_send, moment_recv,
+    final_send, final_recv, final_send_right, final_recv_right, band_send, band_recv, relay_recv,
 ):
     rows, depth = own.shape
     groups = rows // LANE
@@ -28,6 +28,15 @@
     samples = depth * smp_count
     has_left, has_right = var > 0, var < var_count - 1
 
+    def split_of(boundary):
+        between_chips = (boundary + 1) // 2 if var_count == 8 else SPAN // 2
+        return jnp.where(lax.rem(boundary, 2) == 0, SPAN, between_chips)
+
+    columns_out = jnp.where(has_left, split_of(var - 1), 0)
+    rows_in = jnp.where(has_left, split_of(var - 1), SPAN)
+    columns_in = jnp.where(has_right, split_of(var), SPAN)
+    rows_out = columns_in
+
     def peer(step):
         return lax.rem(smp + step, smp_count)
 
@@ -66,6 +75,26 @@
             device_id_type=MESH,
         )
 
+    def before_copy(q):
+        return pltpu.make_async_remote_copy(
+            src_ref=x_ref.at[pl.ds(rows - WIN + q * LANE, LANE)],
+            dst_ref=before.at[pl.ds(q * LANE, LANE)],
+            send_sem=before_send.at[q],
+            recv_sem=before_recv.at[q],
+            device_id=(var + 1, smp),
+            device_id_type=MESH,
+        )
+
+    def lent_copy(q, c):
+        return pltpu.make_async_remote_copy(
+            src_ref=lent.at[q, c],
+            dst_ref=product.at[groups - SPAN + q, :, pl.ds((c + SPAN - q) * LANE, LANE)],
+            send_sem=lent_send.at[q, c],
+            recv_sem=lent_recv.at[q, c],
+            device_id=(var - 1, smp),
+            device_id_type=MESH,
+        )
+
     def final_copy():
         return pltpu.make_async_remote_copy(
             src_ref=final,
@@ -76,10 +105,24 @@
             device_id_type=MESH,
         )
 
-    @pl.when(has_left)
-    def _():
-        for q in range(SPAN):
+    def final_copy_right():
+        return pltpu.make_async_remote_copy(
+            src_ref=final,
+            dst_ref=final_before,
+            send_sem=final_send_right,
+            recv_sem=final_recv_right,
+            device_id=(var + 1, smp),
+            device_id_type=MESH,
+        )
+
+    for q in range(SPAN):
+        @pl.when(q < columns_out)
+        def _():
             after_copy(q).start()
+
+        @pl.when(q >= rows_out)
+        def _():
+            before_copy(q).start()
 
     for g in range(groups):
         loads[g].wait()
@@ -120,27 +163,52 @@
     def _():
         final_copy().start()
 
+    @pl.when(has_right)
+    def _():
+        final_copy_right().start()
+
     def column(row):
         return jnp.broadcast_to(row, (LANE, LANE)).T
 
-    def standardize(held, g, stats):
-        shift = column(stats[pl.ds(g, 1), :])
-        scale = column(stats[pl.ds(groups + g, 1), :])
+    def standardize(held, g, stats, at_stats):
+        shift = column(stats[pl.ds(at_stats, 1), :])
+        scale = column(stats[pl.ds(groups + at_stats, 1), :])
 
         @pl.loop(0, depth // LANE, unroll=4)
         def _(t):
             at = (pl.ds(g * LANE, LANE), pl.ds(pl.multiple_of(t * LANE, LANE), LANE))
             held[at] = ((held[at].astype(jnp.float32) - shift) * scale).astype(jnp.bfloat16)
 
-    def band_copy(g, step):
-        return pltpu.make_async_remote_copy(
-            src_ref=outbox.at[g, peer(step)],
-            dst_ref=inbox.at[g, step - 1],
-            send_sem=band_send.at[g, step - 1],
-            recv_sem=band_recv.at[g, step - 1],
-            device_id=(var, peer(step)),
-            device_id_type=MESH,
-        )
+    inward = jnp.where(smp < smp_count // 2, 1, -1)
+    at_end = (smp == 0) | (smp == smp_count - 1)
+    far = jnp.where(at_end, smp + 3 * inward, smp + 2 * inward)
+    second = jnp.where(at_end, smp + 2 * inward, smp - inward)
+
+    def band_copy(g, slot, share, target, landing, recv_sem):
+        return pltpu.make_async_remote_copy(
+            src_ref=outbox.at[g, share],
+            dst_ref=landing,
+            send_sem=band_send.at[g, slot],
+            recv_sem=recv_sem,
+            device_id=(var, target),
+            device_id_type=MESH,
+        )
+
+    def direct_copy(g, slot, share):
+        return band_copy(g, slot, share, share, inbox.at[g, smp], band_recv.at[g, smp])
+
+    def relay_copy(g):
+        return band_copy(g, 2, far, smp + inward, relayed.at[g], relay_recv.at[g])
+
+    def arrival(g, sender):
+        return band_copy(g, 0, smp, smp + inward, inbox.at[g, sender], band_recv.at[g, sender])
+
+    def relay_group(g):
+        @pl.when(jnp.logical_not(at_end))
+        def _():
+            relay_copy(g).wait_recv()
+            outbox[g, far] = outbox[g, far] + relayed[g]
+            direct_copy(g, 2, far).start()
 
     def finish_group(g):
         width, share = WIN + LANE, WIN // smp_count
@@ -152,8 +220,34 @@
                 value = jnp.where((line >> bit) & 1 == 1, moved, value)
             for part in range(smp_count):
                 outbox[g, part, pl.ds(top, SUB), :] = value[:, part * share : (part + 1) * share]
-        for step in range(1, smp_count):
-            band_copy(g, step).start()
+
+        if g == groups - 1:
+            direct_copy(g, 2, far).start()
+        else:
+            @pl.when(at_end)
+            def _():
+                relay_copy(g).start()
+
+        direct_copy(g, 0, smp + inward).start()
+        direct_copy(g, 1, second).start()
+
+    lane = lax.broadcasted_iota(jnp.int32, (LANE, LANE), 1)
+    line = lax.broadcasted_iota(jnp.int32, (LANE, LANE), 0)
+
+    def finalize(g):
+        arrival(g, smp + inward).wait_recv()
+        arrival(g, second).wait_recv()
+        outbox[g, smp] = outbox[g, smp] + inbox[g, smp + inward] + inbox[g, second]
+
+        @pl.when(jnp.logical_not(at_end) | (g == groups - 1))
+        def _():
+            arrival(g, far).wait_recv()
+            outbox[g, smp] = outbox[g, smp] + inbox[g, far]
+
+        end = column(end_ref[pl.ds(g, 1), :].astype(jnp.float32)).astype(jnp.int32)
+        index = var * rows + g * LANE + line
+        retain = smp * LANE + lane < end - index - 1
+        out_ref[pl.ds(g * LANE, LANE), :] = jnp.where(retain, outbox[g, smp] / samples, 0.0)
 
     def place(value, row, col):
         for i in range(value.shape[0] // LANE):
@@ -168,7 +262,7 @@
         return lax.dot_general(left, right, NT, preferred_element_type=jnp.float32)
 
     for g in range(groups):
-        standardize(own, g, final)
+        standardize(own, g, final, g)
     for g in range(0, groups, 2):
         for c in range(g, min(g + SPAN + 2, groups), 2):
             value = dot(own[pl.ds(g * LANE, 2 * LANE), :], own[pl.ds(c * LANE, 2 * LANE), :])
@@ -176,6 +270,8 @@
         for done in range(g, g + 2):
             if done + SPAN < groups:
                 finish_group(done)
+                if done > 0:
+                    relay_group(done - 1)
 
     @pl.when(has_right)
     def _():
@@ -187,34 +283,83 @@
         after[...] = jnp.zeros_like(after)
 
     for q in range(SPAN):
-        @pl.when(has_right)
-        def _():
-            after_copy(q).wait_recv()
-
-        standardize(after, q, final_after)
         row = groups - SPAN + q
-        value = dot(own[pl.ds(row * LANE, (SPAN - q) * LANE), :], after[pl.ds(q * LANE, LANE), :])
-        place(value, row, groups + q)
+
+        @pl.when(q < columns_in)
+        def _():
+            @pl.when(has_right)
+            def _():
+                after_copy(q).wait_recv()
+
+            standardize(after, q, final_after, q)
+            left = own[pl.ds(row * LANE, (SPAN - q) * LANE), :]
+            place(dot(left, after[pl.ds(q * LANE, LANE), :]), row, groups + q)
+
+        relay_group(row - 1)
+        if q >= 2:
+            @pl.when(columns_in < SPAN)
+            def _():
+                finalize(2 * q - 4)
+                finalize(2 * q - 3)
+
+        for c in range(q + 1):
+            @pl.when(c >= columns_in)
+            def _():
+                lent_copy(q, c).wait_recv()
+
         finish_group(row)
 
-    lane = lax.broadcasted_iota(jnp.int32, (LANE, LANE), 1)
-    line = lax.broadcasted_iota(jnp.int32, (LANE, LANE), 0)
+    @pl.when(has_left)
+    def _():
+        final_copy_right().wait_recv()
+
+    for q in range(SPAN):
+        @pl.when(q >= rows_in)
+        def _():
+            before_copy(q).wait_recv()
+            standardize(before, q, final_before, groups - SPAN + q)
+            value = dot(before[pl.ds(q * LANE, LANE), :], own[pl.ds(0, (q + 1) * LANE), :])
+            for c in range(q + 1):
+                @pl.when(c >= rows_in)
+                def _():
+                    lent[q, c] = value[:, c * LANE : (c + 1) * LANE]
+                    lent_copy(q, c).start()
+
+    @pl.when(columns_in == SPAN)
+    def _():
+        for g in range(groups - SPAN):
+            finalize(g)
+
+    for g in range(groups - SPAN, groups):
+        finalize(g)
+
     for g in range(groups):
-        for step in range(1, smp_count):
-            band_copy(g, step).wait()
-        total = outbox[g, smp]
-        for step in range(1, smp_count):
-            total = total + inbox[g, step - 1]
-        end = column(end_ref[pl.ds(g, 1), :].astype(jnp.float32)).astype(jnp.int32)
-        index = var * rows + g * LANE + line
-        retain = smp * LANE + lane < end - index - 1
-        out_ref[pl.ds(g * LANE, LANE), :] = jnp.where(retain, total / samples, 0.0)
+        for slot in range(3):
+            band_copy(
+                g, slot, far, smp + inward, relayed.at[g], relay_recv.at[g]
+            ).wait_send()
 
     @pl.when(has_left)
     def _():
         final_copy().wait_send()
-        for q in range(SPAN):
+
+    @pl.when(has_right)
+    def _():
+        final_copy_right().wait_send()
+
+    for q in range(SPAN):
+        @pl.when(q < columns_out)
+        def _():
             after_copy(q).wait_send()
+
+        @pl.when(q >= rows_out)
+        def _():
+            before_copy(q).wait_send()
+
+        for c in range(q + 1):
+            @pl.when((q >= rows_in) & (c >= rows_in))
+            def _():
+                lent_copy(q, c).wait_send()
 
 
 def local(dosages, window_end):
@@ -231,22 +376,33 @@
         scratch_shapes=[
             pltpu.VMEM((rows, depth), jnp.bfloat16),
             pltpu.VMEM((WIN, depth), jnp.bfloat16),
+            pltpu.VMEM((WIN, depth), jnp.bfloat16),
+            pltpu.VMEM((SPAN, SPAN, LANE, LANE), jnp.float32),
             pltpu.VMEM((groups, LANE, WIN + LANE), jnp.float32),
             pltpu.VMEM((groups, smp_count, LANE, share), jnp.float32),
-            pltpu.VMEM((groups, smp_count - 1, LANE, share), jnp.float32),
+            pltpu.VMEM((groups, smp_count, LANE, share), jnp.float32),
+            pltpu.VMEM((groups, LANE, share), jnp.float32),
             pltpu.VMEM((2 * groups, LANE), jnp.float32),
             pltpu.VMEM((smp_count - 1, 2 * groups, LANE), jnp.float32),
+            pltpu.VMEM((2 * groups, LANE), jnp.float32),
             pltpu.VMEM((2 * groups, LANE), jnp.float32),
             pltpu.VMEM((2 * groups, LANE), jnp.float32),
             dma((groups,)),
             dma((SPAN,)),
             dma((SPAN,)),
+            dma((SPAN,)),
+            dma((SPAN,)),
+            dma((SPAN, SPAN)),
+            dma((SPAN, SPAN)),
             dma((smp_count - 1,)),
             dma((smp_count - 1,)),
             dma,
             dma,
-            dma((groups, smp_count - 1)),
-            dma((groups, smp_count - 1)),
+            dma,
+            dma,
+            dma((groups, 3)),
+            dma((groups, smp_count)),
+            dma((groups,)),
         ],
         compiler_params=pltpu.CompilerParams(
             collective_id=0, has_side_effects=True, vmem_limit_bytes=48 * 1024 * 1024

time: 69.9 us -> 60.9 us (0.87); the launches traced: 68.9 us -> 60.7 us
  Pallas kernels: 67.4 us -> 59.3 us
    pallas_call x1, Pallas kernels: 67.4 us -> 59.3 us  [local(): pl.pallas_call(kernel, out_shape=jax.ShapeDtypeStruct((rows, share), jnp....]
where the time goes in v2:
time: 60.9 us; the launch traced here: 60.7 us
  Pallas kernels  59.3 us (97%)
  local copies, waits for them, and re-layouts  1.48 us (2%)
    pallas_call x1, Pallas kernels, local(): pl.pallas_call(kernel, out_shape=jax.ShapeDtypeStruct((rows, share), jnp....  59.3 us
    unnamed x3, local copies, waits for them, and re-layouts  1.48 us

profile of v2, /device:TPU:5, one launch (start us, length us, event | category | flops | bytes accessed | tf_op | source)
XLA Modules:
  0.0 60.7 jit_solution(14732995398633922214)
XLA Ops:
  0.0 0.0 copy-start
  0.0 0.7 %copy-done = s32[1024]{0:T(1024)S(1)} copy-done((s32[1024]{0:T(1024)S(1)}, s32[1024]{0:T(1024)}, u32[]{:S(2)}) %copy-start) | copy-done | bytes 4120
  0.7 59.3 %shard_map.28 = f32[1024,128]{1,0:T(8,128)S(1)} custom-call(bf16[1024,4096]{1,0:T(8,128)(2,1)} %x_ref.1, s32[8,128]{1,0:T(8,128)S(1)} %bitcast.1), custom_call_target="tpu_custom_call" | custom-call | tf_op jit(solution)/shard_map/pallas_call | solution.py:371
  59.9 0.8 %copy.4 = f32[1024,128]{1,0:T(8,128)} copy(f32[1024,128]{1,0:T(8,128)S(1)} %shard_map.28) | data formatting | bytes 1048576
Async XLA Ops:
  0.0 0.7 %copy-start = (s32[1024]{0:T(1024)S(1)}, s32[1024]{0:T(1024)}, u32[]{:S(2)}) copy-start(s32[1024]{0:T(1024)} %param.3) | copy-start | bytes 12292

commit v3 on v2

--- a/solution.py
+++ b/solution.py
@@ -261,9 +261,12 @@
     def dot(left, right):
         return lax.dot_general(left, right, NT, preferred_element_type=jnp.float32)
 
-    for g in range(groups):
-        standardize(own, g, final, g)
+    scaled = 0
     for g in range(0, groups, 2):
+        needed = min(g + SPAN + 2, groups)
+        for c in range(scaled, needed):
+            standardize(own, c, final, c)
+        scaled = needed
         for c in range(g, min(g + SPAN + 2, groups), 2):
             value = dot(own[pl.ds(g * LANE, 2 * LANE), :], own[pl.ds(c * LANE, 2 * LANE), :])
             place(value, g, c)
@@ -299,8 +302,8 @@
         if q >= 2:
             @pl.when(columns_in < SPAN)
             def _():
-                finalize(2 * q - 4)
-                finalize(2 * q - 3)
+                for g in range(2) if q == 2 else range(2, SPAN + 2):
+                    finalize(g)
 
         for c in range(q + 1):
             @pl.when(c >= columns_in)
@@ -327,10 +330,10 @@
 
     @pl.when(columns_in == SPAN)
     def _():
-        for g in range(groups - SPAN):
+        for g in range(groups - 2):
             finalize(g)
 
-    for g in range(groups - SPAN, groups):
+    for g in range(groups - 2, groups):
         finalize(g)
 
     for g in range(groups):

time: 60.9 us -> 60.3 us (level)
  Pallas kernels: 59.3 us -> 58.6 us
    pallas_call x1, Pallas kernels: 59.3 us -> 58.6 us  [local(): pl.pallas_call(kernel, out_shape=jax.ShapeDtypeStruct((rows, share), jnp....]
where the time goes in v3:
time: 60.3 us; the launch traced here: 60.1 us
  Pallas kernels  58.6 us (97%)
  local copies, waits for them, and re-layouts  1.48 us (2%)
    pallas_call x1, Pallas kernels, local(): pl.pallas_call(kernel, out_shape=jax.ShapeDtypeStruct((rows, share), jnp....  58.6 us
    unnamed x3, local copies, waits for them, and re-layouts  1.48 us

profile of v3, /device:TPU:5, one launch (start us, length us, event | category | flops | bytes accessed | tf_op | source)
XLA Modules:
  0.0 60.1 jit_solution(7151901745015198639)
XLA Ops:
  0.0 0.0 copy-start
  0.0 0.7 %copy-done = s32[1024]{0:T(1024)S(1)} copy-done((s32[1024]{0:T(1024)S(1)}, s32[1024]{0:T(1024)}, u32[]{:S(2)}) %copy-start) | copy-done | bytes 4120
  0.7 58.6 %shard_map.28 = f32[1024,128]{1,0:T(8,128)S(1)} custom-call(bf16[1024,4096]{1,0:T(8,128)(2,1)} %x_ref.1, s32[8,128]{1,0:T(8,128)S(1)} %bitcast.1), custom_call_target="tpu_custom_call" | custom-call | tf_op jit(solution)/shard_map/pallas_call | solution.py:374
  59.3 0.8 %copy.4 = f32[1024,128]{1,0:T(8,128)} copy(f32[1024,128]{1,0:T(8,128)S(1)} %shard_map.28) | data formatting | bytes 1048576
Async XLA Ops:
  0.0 0.7 %copy-start = (s32[1024]{0:T(1024)S(1)}, s32[1024]{0:T(1024)}, u32[]{:S(2)}) copy-start(s32[1024]{0:T(1024)} %param.3) | copy-start | bytes 12292
